TPU v7x, 128 devices: a whole 4x4x4 slice. The times are simulated.
128 devices in a mesh: dp: 8 (over x, z_hi), row: 16 (over y, z_lo, core).
Axes of the slice: x: 4, y: 4, z: 4 (z_hi: 2, z_lo: 2; z = z_hi * 2 + z_lo), core: 2. Of those that a mesh axis runs over, the one named last changes fastest.
Arguments:
- pair_rep: bfloat16 [8, 384, 384, 128], P('dp', 'row'), may hold values from -6 to 6
- grad_out: bfloat16 [8, 384, 384, 128], P('dp', 'row'), may hold values from -6 to 6
- crop_len: int32 [8], P('dp'), may hold values from 288 to 384, as said below
- ln_gain: float32 [128], replicated, may hold values from 0.25 to 1.75
- ln_bias: float32 [128], replicated, may hold values from -3 to 3
- w_proj: bfloat16 [128, 512], replicated, may hold values from -0.5 to 0.5
- gate_bias: float32 [128], replicated, may hold values from -4 to 4
- w_bias: bfloat16 [128, 4], replicated, may hold values from -0.5 to 0.5
- w_out: bfloat16 [128, 128], replicated, may hold values from -0.5 to 0.5
Outputs:
- pair_grad: bfloat16 [8, 384, 384, 128], P('dp', 'row')
- proj_grad: float32 [128, 512], replicated
- gate_bias_grad: float32 [128], replicated
- bias_w_grad: float32 [128, 4], replicated
- out_w_grad: float32 [128, 128], replicated
- gain_grad: float32 [128], replicated
- shift_grad: float32 [128], replicated
Inputs may be any that keep to these rules, and one draw needn't show every extreme that they name: `crop_len`: every crop is padded to 384; in every draw one crop fills all 384 residues and one has 288.
All inputs are finite; a program needn't handle non-finite values.
Results may differ from a plain program's by a relative error of at most 0.025.
Values may be sent and summed in bfloat16 or wider, within the bound.
No kernel may reach another device: no remote copies, remote signals or barrier semaphores. Data moves between devices by JAX's collectives and lax.ppermute only.
A program may use at most 128 MiB of HBM per device.

v0:
```python
import functools
import math

import jax
import jax.numpy as jnp
from jax import lax
from jax.experimental import pallas as pl
from jax.experimental.pallas import tpu as pltpu
from jax.sharding import PartitionSpec as P

F32, BF = jnp.float32, jnp.bfloat16
EPSILON = 1e-05
LOG2E = 1.4426950408889634
LN2 = 0.6931471805599453
NN = (((1,), (0,)), ((), ()))
NT = (((1,), (1,)), ((), ()))
TN = (((0,), (0,)), ((), ()))
MIB = 2**20
DEAD = -1e30
CHUNKS = (6, 9, 9)
SAFE = 1e28
GROUPS = (3, 9, 9)
SHARES = 4
SLOTS, STAGES, LAG = 4, 6, 2


def dot(a, b, dims=NN):
    return lax.dot_general(a, b, dims, preferred_element_type=F32)


def halves(a):
    high = a.astype(BF)
    return jnp.concatenate([high, (a - high.astype(F32)).astype(BF)], axis=1)


def lane_mean(a):
    channels = a.shape[1]
    a = a if a.dtype == BF else halves(a)
    return dot(a, jnp.full((a.shape[1], channels), 1.0 / channels, BF))


def norm_parts(x):
    centered = x.astype(F32) - lane_mean(x)
    scale = lax.rsqrt(lane_mean(centered * centered) + EPSILON)
    return centered * scale, scale


def fold_rows(a):
    return jnp.sum(a.reshape(a.shape[0] // 8, 8, a.shape[1]), axis=0)


def logits_kernel(heads, pair_ref, gain_ref, shift_ref, wbt_ref, out_ref):
    rows, n, channels = pair_ref.shape
    xhat, _ = norm_parts(pair_ref[...].astype(F32).reshape(rows * n, channels).astype(BF))
    normed = (xhat * gain_ref[...] + shift_ref[...]).astype(BF)
    logits = dot(wbt_ref[...], normed, NT)
    for r in range(rows):
        for h in range(heads):
            for t in range(n // channels):
                start = r * n + t * channels
                piece = logits[h : h + 1, start : start + channels]
                out_ref[h * (n // channels) + t, r : r + 1, :] = piece


def send_kernel(start, count, pair_ref, cot_ref, *refs):
    out = refs[-1]
    block, rows = out.shape[0], pair_ref.shape[0]
    skip = out.shape[1] - 2 * count
    if skip:
        for s in range(block):
            out[s, :skip] = refs[0][...].astype(BF)
    for a, ref in enumerate((pair_ref, cot_ref)):
        cells = ref[...].astype(F32)
        for s in range(block):
            first = s * rows + start
            own = jnp.swapaxes(cells[:, first : first + count], 0, 1)
            out[s, skip + a * count : skip + (a + 1) * count] = own.astype(BF)


def columns_kernel(heads, first, last, col0, cols, group, len_ref, own_ref, cells_ref, *refs):
    if not first:
        (bias_ref, bacc_in, wacc_in, sacc_in), refs = refs[:4], refs[4:]
    if not first and not last:
        early_ref, refs = refs[0], refs[1:]
    gain_ref, shift_ref, wp_ref, wpt_ref, gb_ref, wot_ref = refs[:6]
    refs = refs[6:]
    out_ref, sacc_ref = refs[:2]
    refs = refs[2:]
    if not last:
        (bacc_ref, wacc_ref), refs = refs[:2], refs[2:]
    if first:
        bias_ref, refs = refs[0], refs[1:]
    e_all, ds_all, kbd_all, vaug_all, off_ref, sems = refs[:6]
    refs = refs[6:]
    if last:
        bacc_ref, wacc_ref = refs
    step = pl.program_id(0)
    n, channels = bacc_ref.shape[0], wp_ref.shape[0]
    size, thirds, src = channels // heads, n // channels, cells_ref.shape[0]
    slots = heads * thirds
    skip_in = slots if first else 0
    skip_out = slots + SHARES if last else out_ref.shape[1] - cols
    lane = lax.broadcasted_iota(jnp.int32, (1, channels), 1)
    masks = [jnp.where(lane // size == h, 1.0, 0.0).astype(BF) for h in range(heads)]
    length = len_ref[0]

    def total_copy():
        return pltpu.make_async_copy(bacc_in, bacc_ref, sems.at[0])

    def early_copy():
        return pltpu.make_async_copy(early_ref, out_ref.at[:, :skip_out], sems.at[1])

    def begin():
        if first:
            bacc_ref[...] = jnp.zeros_like(bacc_ref)
            wacc_ref[...] = jnp.zeros_like(wacc_ref)
            sacc_ref[...] = jnp.zeros_like(sacc_ref)
        else:
            total_copy().start()
            wacc_ref[...] = wacc_in[...]
            sacc_ref[...] = sacc_in[...]

    @pl.when(step == 0)
    def _():
        begin()
        if first:
            kpos = lax.broadcasted_iota(jnp.int32, (1, n), 1)
            for h in range(heads):
                for t in range(thirds):
                    plane = cells_ref[:, h * thirds + t].astype(F32).reshape(n, channels)
                    bias_ref[t * channels : (t + 1) * channels, h * n : (h + 1) * n] = jnp.where(
                        kpos < length, plane.T * LOG2E, DEAD
                    )
        elif not last:
            early_copy().start()
        off_ref[...] = jnp.zeros_like(off_ref)
        for h in range(heads):
            for u in range(SLOTS):
                vaug_all[u, h * n : (h + 1) * n, channels:] = jnp.broadcast_to(masks[h], (n, channels))

    def column(j, shifted, slot, wait=False):
        e_ref, ds_ref, kbd, vaug = e_all.at[slot], ds_all.at[slot], kbd_all.at[slot], vaug_all.at[slot]
        xhat, _ = norm_parts(cells_ref[:, skip_in + j].astype(F32).reshape(n, channels).astype(BF))
        normed_f = xhat * gain_ref[...] + shift_ref[...]
        proj = dot(normed_f.astype(BF), wp_ref[...])
        q_f = proj[:, :channels] * (LOG2E / math.sqrt(size))
        k = proj[:, channels : 2 * channels].astype(BF)
        v = proj[:, 2 * channels : 3 * channels].astype(BF)
        gate = jax.nn.sigmoid(proj[:, 3 * channels :] + gb_ref[...])
        for h in range(heads):
            kbd[h * n : (h + 1) * n, :] = k * masks[h]
            vaug[h * n : (h + 1) * n, :channels] = v * masks[h]
        live = lax.broadcasted_iota(jnp.int32, (n, 1), 0) < length
        live = live & (own_ref[0] + col0 + j < length)
        cot = cells_ref[:, skip_in + cols + j].astype(F32).reshape(n, channels)
        cot = jnp.where(live, cot, 0.0).astype(BF)
        d_out = dot(cot, wot_ref[...])

        yield
        scores = dot(q_f.astype(BF), kbd[...], NT) + bias_ref[...]
        if shifted:
            for h in range(heads):
                part = scores[:, h * n : (h + 1) * n]
                part = jnp.exp2(part - jnp.max(part, axis=1, keepdims=True))
                e_ref[:, h * n : (h + 1) * n] = part.astype(BF)
        else:
            e_ref[...] = jnp.exp2(scores).astype(BF)
        yield
        summed = dot(e_ref[...], vaug[...])
        total = summed[:, channels:]
        if not shifted:
            fits = (total > 1.0 / SAFE) & (total < SAFE)
            off_ref[...] += fold_rows(jnp.where(fits, 0.0, 1.0))
        recip = 1.0 / total
        att = summed[:, :channels] * recip
        d_att = d_out * gate
        d_gate = d_att * att * (1.0 - gate)
        d_att_b = (d_att * recip).astype(BF)
        d_att_f = d_att_b.astype(F32)
        gi = lax.broadcasted_iota(jnp.int32, (2 * channels, channels), 0) % channels
        gj = lax.broadcasted_iota(jnp.int32, (2 * channels, channels), 1)
        group = jnp.where((gi // size == gj // size) & (gj % size < 2), -1.0, 0.0).astype(BF)
        row_dot = dot(halves(d_att_f * att), group)
        row_hi = row_dot.astype(BF).astype(F32)
        row_lanes = jnp.where(lane % size == 0, row_hi, row_dot - row_hi).astype(BF)
        yield
        d_probs = dot(jnp.concatenate([d_att_b, row_lanes], axis=1), vaug[...], NT)
        ds = e_ref[...].astype(F32) * d_probs
        if wait:
            total_copy().wait()
        bacc_ref[...] += ds
        ds_ref[...] = ds.astype(BF)
        yield
        d_query = dot(ds_ref[...], kbd[...]) * (1.0 / math.sqrt(size))
        q_t, d_att_t = q_f.T.astype(BF), d_att_f.T.astype(BF)
        dk_t, dv_t = [], []
        for p in range(heads // 2):
            rows = slice(2 * p * size, 2 * (p + 1) * size)
            lanes = slice(2 * p * n, 2 * (p + 1) * n)
            both = dot(q_t[rows], ds_ref[:, lanes])
            dk_t += [both[:size, :n], both[size:, n:]]
            both = dot(d_att_t[rows], e_ref[:, lanes])
            dv_t += [both[:size, :n], both[size:, n:]]
        d_key = (jnp.concatenate(dk_t, axis=0) * LN2).T
        d_value = jnp.concatenate(dv_t, axis=0).T
        yield
        d_proj = jnp.concatenate([g.astype(BF) for g in (d_query, d_key, d_value, d_gate)], axis=1)
        dn = dot(d_proj, wpt_ref[...])
        out_ref[:, skip_out + j] = dn.reshape(src, n // src, channels).astype(BF)
        gated = gate * att
        wacc_ref[:, : 4 * channels] += dot(normed_f.T.astype(BF), d_proj)
        wacc_ref[:, 4 * channels :] += dot(gated.T.astype(BF), cot)
        sacc_ref[0] += fold_rows(d_gate)
        sacc_ref[1] += fold_rows(dn * xhat)
        sacc_ref[2] += fold_rows(dn)

    ahead = [
        column(step * group + u, False, u % SLOTS, not first and u == 0) for u in range(group)
    ]
    for turn in range(STAGES + LAG * (group - 1)):
        for u in range(group):
            if LAG * u <= turn < STAGES + LAG * u:
                next(ahead[u], None)

    @pl.when(step == cols // group - 1)
    def _():
        @pl.when(jnp.max(off_ref[...]) > 0.0)
        def _():
            begin()
            if not first:
                total_copy().wait()

            @pl.loop(0, cols)
            def _(j):
                for _ in column(j, True, 0):
                    pass

        if not first and not last:
            early_copy().wait()
        if last:
            for h in range(heads):
                for t in range(thirds):
                    plane = bacc_ref[t * channels : (t + 1) * channels, h * n : (h + 1) * n].T
                    out_ref[:, h * thirds + t] = plane.reshape(src, n // src, channels).astype(BF)
            terms = []
            for w in range(5):
                part = wacc_ref[:, w * channels : (w + 1) * channels].reshape(src, -1, channels)
                terms.append(part.astype(BF).astype(F32))
                terms.append(part - terms[-1])
            terms += [jnp.zeros_like(terms[0])] * 2
            for w in range(SHARES):
                three = jnp.concatenate(terms[3 * w : 3 * w + 3], axis=1)
                out_ref[:, slots + w] = three.astype(BF)


def whole(shape):
    return pl.BlockSpec(shape, lambda j: (0,) * len(shape))


def columns_call(first, last, col0, cols, group, length, own, moved, state, weights, heads):
    src, _, rows, channels = moved.shape
    n = src * rows
    slots = heads * n // channels
    smem = pl.BlockSpec(memory_space=pltpu.SMEM)
    plane = jax.ShapeDtypeStruct((n, heads * n), F32)
    wide = jax.ShapeDtypeStruct((channels, 5 * channels), F32)
    outs = [
        jax.ShapeDtypeStruct((src, cols + (slots + SHARES if last else col0), rows, channels), BF),
        jax.ShapeDtypeStruct((3, 8, channels), F32),
    ]
    outs += ([] if last else [plane, wide]) + ([plane] if first else [])
    inputs = (moved, *state, *weights)
    anywhere = pl.BlockSpec(memory_space=pl.ANY)
    in_specs = [smem, smem] + [whole(a.shape) for a in inputs]
    if not first:
        in_specs[4] = anywhere
    if len(state) > 4:
        in_specs[7] = anywhere
    return pl.pallas_call(
        functools.partial(columns_kernel, heads, first, last, col0, cols, group),
        grid=(cols // group,),
        in_specs=in_specs,
        out_specs=[whole(o.shape) for o in outs],
        out_shape=outs,
        scratch_shapes=[
            pltpu.VMEM((SLOTS, n, heads * n), BF),
            pltpu.VMEM((SLOTS, n, heads * n), BF),
            pltpu.VMEM((SLOTS, heads * n, channels), BF),
            pltpu.VMEM((SLOTS, heads * n, 2 * channels), BF),
            pltpu.VMEM((8, channels), F32),
            pltpu.SemaphoreType.DMA((2,)),
        ]
        + ([pltpu.VMEM(o.shape, F32) for o in (plane, wide)] if last else []),
        compiler_params=pltpu.CompilerParams(
            vmem_limit_bytes=56 * MIB, dimension_semantics=("arbitrary",)
        ),
        cost_estimate=pl.CostEstimate(
            flops=cols * 4 * 10**9, bytes_accessed=cols * n * channels * 6, transcendentals=0
        ),
    )(length, own, *inputs)


def side_kernel(heads, pair_ref, parts_ref, gain_ref, shift_ref, wbt_ref, sacc_ref, sum_ref, share_ref):
    rows, n, channels = pair_ref.shape
    thirds = n // channels
    slots = heads * thirds
    total = jnp.sum(parts_ref[:, :slots].astype(F32), axis=0).astype(BF).astype(F32)
    for h in range(heads):
        for t in range(thirds):
            sum_ref[h, :, t * channels : (t + 1) * channels] = total[h * thirds + t]
    terms = []
    for w in range(SHARES):
        part = jnp.sum(parts_ref[:, slots + w].astype(F32), axis=0)
        terms += [part[:8], part[8:16], part[16:24]]
    for w in range(5):
        share_ref[w] = terms[2 * w] + terms[2 * w + 1]
    stats = jnp.zeros((heads, 2 * channels), F32)
    flat = jnp.zeros((heads, n), F32)
    for r in range(rows):
        xhat, _ = norm_parts(pair_ref[r])
        normed = (xhat * gain_ref[...] + shift_ref[...]).astype(BF)
        own = sum_ref[:, r, :]
        flat = flat + own
        stats = stats + dot(own.astype(BF), jnp.concatenate([normed, xhat.astype(BF)], axis=1))
    wide = wbt_ref[...].astype(F32)
    share_ref[5, 0:1, :] = jnp.sum(sacc_ref[0], axis=0, keepdims=True)
    gain_part = wide * stats[:, channels:]
    gain_all = jnp.sum(sacc_ref[1], axis=0, keepdims=True)
    share_ref[5, 1:2, :] = gain_all + jnp.sum(gain_part, axis=0, keepdims=True)
    shift_part = wide * jnp.sum(flat, axis=1, keepdims=True)
    shift_all = jnp.sum(sacc_ref[2], axis=0, keepdims=True)
    share_ref[5, 2:3, :] = shift_all + jnp.sum(shift_part, axis=0, keepdims=True)
    share_ref[5, 3 : 3 + heads, :] = stats[:, :channels]
    share_ref[5, 3 + heads :, :] = jnp.zeros((5 - heads, channels), F32)


def norm_back_kernel(first, pair_ref, sums_ref, gain_ref, wbt_ref, *refs):
    parts, out_ref, side_ref = refs[:2], refs[-2], refs[-1]
    rows, cols, channels = pair_ref.shape
    heads, n = sums_ref.shape[0], sums_ref.shape[2]
    step = pl.program_id(0)

    @pl.when(step == 0)
    def _():
        none = jnp.zeros((8 - heads, n), F32)
        span = side_ref.shape[1]
        for r in range(rows):
            own = jnp.concatenate([sums_ref[:, r, :], none], axis=0).T
            own = own[first * cols : first * cols + span, :heads].astype(BF)
            side_ref[r] = dot(own, wbt_ref[...])

    pieces = []
    for s in range(cols // rows):
        for ref, w in zip(parts, (sum(CHUNKS[:-1]), CHUNKS[-1])):
            pieces.append(ref[s, ref.shape[1] - w :].astype(F32))
    main = jnp.swapaxes(jnp.concatenate(pieces, axis=0), 0, 1)
    side = side_ref[:, pl.ds(pl.multiple_of(step * cols, cols), cols), :]
    d_normed = (main + side).astype(BF).astype(F32).reshape(rows * cols, channels)
    cells = pair_ref[...].astype(F32).reshape(rows * cols, channels).astype(BF)
    xhat, scale = norm_parts(cells)
    g = d_normed * gain_ref[...]
    dx = scale * (g - lane_mean(g) - xhat * lane_mean(g * xhat))
    out_ref[...] = dx.reshape(rows, cols, channels).astype(BF)


def final_kernel(heads, size, told_ref, proj_ref, gate_ref, biasw_ref, outw_ref, gain_ref, shift_ref):
    channels = told_ref.shape[-1]
    scale = 1.0 / size
    for w in range(5):
        part = told_ref[:, w].reshape(channels, channels) * scale
        if w < 4:
            proj_ref[:, w * channels : (w + 1) * channels] = part
        else:
            outw_ref[...] = part
    small = jnp.sum(told_ref[:, 5], axis=0) * scale
    gate_ref[...] = small[0:1]
    gain_ref[...] = small[1:2]
    shift_ref[...] = small[2:3]
    biasw_ref[...] = small[3 : 3 + heads]


def body(pair_rep, grad_out, crop_len, ln_gain, ln_bias, w_proj, gate_bias, w_bias, w_out):
    pair, cot = pair_rep[0], grad_out[0]
    rows, n, channels = pair.shape
    heads = w_bias.shape[1]
    src = n // rows
    slots = heads * n // channels
    own = (lax.axis_index("row") * rows).astype(jnp.int32).reshape(1)
    gain, shift = ln_gain.reshape(1, -1), ln_bias.reshape(1, -1)
    wbt = w_bias.T
    weights = (gain, shift, w_proj, w_proj.T, gate_bias.reshape(1, -1), w_out.T)

    def exchange(a, axis="row"):
        return lax.all_to_all(a, axis, 0, 0)

    def tell(a, axis):
        return exchange(jnp.broadcast_to(a[None], (lax.axis_size(axis), *a.shape)), axis)

    block = 2
    tile = block * rows
    lines = 8
    plane = pl.pallas_call(
        functools.partial(logits_kernel, heads),
        grid=(rows // lines,),
        in_specs=[pl.BlockSpec((lines, n, channels), lambda j: (j, 0, 0))]
        + [whole(a.shape) for a in (gain, shift, wbt)],
        out_specs=pl.BlockSpec((slots, lines, channels), lambda j: (0, j, 0)),
        out_shape=jax.ShapeDtypeStruct((slots, rows, channels), F32),
        compiler_params=pltpu.CompilerParams(vmem_limit_bytes=60 * MIB),
    )(pair, gain, shift, wbt)
    many = src // 2
    cells = pl.BlockSpec((rows, many * rows, channels), lambda j: (0, j, 0))

    def send(start, count, extra):
        deep = 2 * count + sum(a.shape[0] for a in extra)
        return pl.pallas_call(
            functools.partial(send_kernel, start, count),
            grid=(src // many,),
            in_specs=[cells, cells] + [whole(a.shape) for a in extra],
            out_specs=pl.BlockSpec((many, deep, rows, channels), lambda j: (j, 0, 0, 0)),
            out_shape=jax.ShapeDtypeStruct((src, deep, rows, channels), BF),
            compiler_params=pltpu.CompilerParams(vmem_limit_bytes=60 * MIB),
            cost_estimate=pl.CostEstimate(
                flops=5 * 10**9, bytes_accessed=3 * pair.size, transcendentals=0
            ),
        )(pair, cot, *extra)

    starts = [sum(CHUNKS[:c]) for c in range(len(CHUNKS))]
    sent = [send(a, w, (plane,) if a == 0 else ()) for a, w in zip(starts, CHUNKS)]
    moved = [exchange(a) for a in sent]
    state, back = (), []
    for c, (start, width, group, piece) in enumerate(zip(starts, CHUNKS, GROUPS, moved)):
        first, last = c == 0, c == len(CHUNKS) - 1
        out, sacc, *rest = columns_call(
            first, last, start, width, group, crop_len, own, piece, state, weights, heads
        )
        if not last:
            plane = rest[2] if first else state[0]
            state = (plane, rest[0], rest[1], sacc)
            if c == len(CHUNKS) - 2:
                early = exchange(out)
            else:
                state += (out,)
    out, early = lax.optimization_barrier((out, early))
    bundle = exchange(out)
    back = (early, bundle)

    sums, share = pl.pallas_call(
        functools.partial(side_kernel, heads),
        grid=(1,),
        in_specs=[
            whole(pair.shape),
            pl.BlockSpec((src, slots + SHARES, rows, channels), lambda j: (0, 0, 0, 0)),
        ]
        + [whole(a.shape) for a in (gain, shift, wbt, sacc)],
        out_specs=[whole((heads, rows, n)), whole((6, 8, channels))],
        out_shape=[
            jax.ShapeDtypeStruct((heads, rows, n), F32),
            jax.ShapeDtypeStruct((6, 8, channels), F32),
        ],
        compiler_params=pltpu.CompilerParams(vmem_limit_bytes=40 * MIB),
    )(pair, bundle, gain, shift, wbt, sacc)
    def norm_back(first, steps, *written):
        place = lambda j: (0, j + first, 0)
        inputs = (pair, sums, gain, wbt, *back)
        return pl.pallas_call(
            functools.partial(norm_back_kernel, first),
            grid=(steps,),
            in_specs=[pl.BlockSpec((rows, tile, channels), place)]
            + [whole(a.shape) for a in (sums, gain, wbt)]
            + [pl.BlockSpec((block, *a.shape[1:]), lambda j: (j + first, 0, 0, 0)) for a in back]
            + [pl.BlockSpec(memory_space=pl.ANY)] * len(written),
            out_specs=pl.BlockSpec((rows, tile, channels), place),
            out_shape=jax.ShapeDtypeStruct(pair.shape, BF),
            scratch_shapes=[pltpu.VMEM((rows, steps * tile, channels), F32)],
            input_output_aliases={len(inputs): 0} if written else {},
            compiler_params=pltpu.CompilerParams(vmem_limit_bytes=60 * MIB),
            cost_estimate=pl.CostEstimate(
                flops=6 * 10**9, bytes_accessed=2 * pair.size, transcendentals=0
            ),
        )(*inputs, *written)

    blocks = n // tile
    share = tell(share, "dp")
    pair_grad = norm_back(0, blocks // 2)
    share, pair_grad = lax.optimization_barrier((share, pair_grad))
    told = tell(jnp.sum(share, axis=0), "row")
    pair_grad = norm_back(blocks // 2, blocks - blocks // 2, pair_grad)
    proj, gate, biasw, outw, gain_sum, shift_sum = pl.pallas_call(
        functools.partial(final_kernel, heads, n),
        out_shape=[
            jax.ShapeDtypeStruct(s, F32)
            for s in (
                w_proj.shape,
                (1, channels),
                (heads, channels),
                w_out.shape,
                (1, channels),
                (1, channels),
            )
        ],
    )(told)
    return (
        pair_grad[None],
        proj,
        gate.reshape(-1),
        biasw.T,
        outw,
        gain_sum.reshape(-1),
        shift_sum.reshape(-1),
    )


def solution(mesh):
    placed = (
        P("dp", "row", None, None),
        P("dp", "row", None, None),
        P("dp"),
        P(),
        P(),
        P(),
        P(),
        P(),
        P(),
    )
    return jax.shard_map(
        body,
        mesh=mesh,
        in_specs=placed,
        out_specs=(P("dp", "row", None, None), P(), P(), P(), P(), P(), P()),
        check_vma=False,
    )
```

profile of v0, /device:TPU:1, one launch (start us, length us, event | category | flops | bytes accessed | tf_op | source)
XLA Modules:
  0.0 218.1 jit_solution(27110322591069149)
XLA Ops:
  0.6 5.4 %shard_map.145.refs_0_ = f32[12,24,128]{2,1,0:T(8,128)} custom-call(bf16[24,384,128]{2,1,0:T(8,128)(2,1)} %bitcast.14, f32[1,128]{1,0:T(1,128)} %bitcast.30, f32[1,128]{1,0:T(1,128)} %bitcast.25, bf16[4,128]{1,0:T(4,128)(2,1)} %bitcast.21), custom_call_target="tpu_custom_call" | custom-call | tf_op jit(solution)/shard_map/pallas_call | solution.py:402
  6.0 3.8 %shard_map.146 = bf16[16,24,24,128]{3,2,1,0:T(8,128)(2,1)} custom-call(bf16[24,384,128]{2,1,0:T(8,128)(2,1)} %bitcast.15, bf16[24,384,128]{2,1,0:T(8,128)(2,1)} %bitcast.43, f32[12,24,128]{2,1,0:T(8,128)} %shard_map.145.refs_0_), custom_call_target="tpu_custom_call" | custom-call | flops 5000000000 | bytes 3538944 | tf_op jit(solution)/shard_map/pallas_call | solution.py:416
  9.8 7.5 %all-to-all-start.1 = ((bf16[16,24,24,128]{3,2,1,0:T(8,128)(2,1)}), bf16[16,24,24,128]{3,2,1,0:T(8,128)(2,1)S(1)}, u32[]{:S(2)}, u32[]{:S(2)}) async-start(bf16[16,24,24,128]{3,2,1,0:T(8,128)(2,1)} %shard_map.146), calls=%async_computation.1 | async-start | bytes 4718592 | tf_op jit(solution)/shard_map/all_to_all | solution.py:394
  17.3 0.8 copy.17
  19.4 3.9 %shard_map.148 = bf16[16,18,24,128]{3,2,1,0:T(8,128)(2,1)} custom-call(bf16[24,384,128]{2,1,0:T(8,128)(2,1)} %bitcast.16, bf16[24,384,128]{2,1,0:T(8,128)(2,1)} %bitcast.44), custom_call_target="tpu_custom_call" | custom-call | flops 5000000000 | bytes 3538944 | tf_op jit(solution)/shard_map/pallas_call | solution.py:416
  23.4 3.9 %shard_map.144 = bf16[16,18,24,128]{3,2,1,0:T(8,128)(2,1)} custom-call(bf16[24,384,128]{2,1,0:T(8,128)(2,1)} %bitcast.17, bf16[24,384,128]{2,1,0:T(8,128)(2,1)} %bitcast.45), custom_call_target="tpu_custom_call" | custom-call | flops 5000000000 | bytes 3538944 | tf_op jit(solution)/shard_map/pallas_call | solution.py:416
  27.3 20.2 %all-to-all-done.1.cells_ref = bf16[16,24,24,128]{3,2,1,0:T(8,128)(2,1)S(1)} async-done(((bf16[16,24,24,128]{3,2,1,0:T(8,128)(2,1)}), bf16[16,24,24,128]{3,2,1,0:T(8,128)(2,1)S(1)}, u32[]{:S(2)}, u32[]{:S(2)}) %all-to-all-start.1) | async-done | bytes 2359328 | tf_op jit(solution)/shard_map/all_to_all | solution.py:394
  47.5 6.3 %all-to-all-start.2 = ((bf16[16,18,24,128]{3,2,1,0:T(8,128)(2,1)}), bf16[16,18,24,128]{3,2,1,0:T(8,128)(2,1)}, u32[]{:S(2)}, u32[]{:S(2)}) async-start(bf16[16,18,24,128]{3,2,1,0:T(8,128)(2,1)} %shard_map.148), calls=%async_computation.2 | async-start | bytes 3538944 | tf_op jit(solution)/shard_map/all_to_all | solution.py:394
  53.8 21.4 %shard_map.147 = (bf16[16,6,24,128]{3,2,1,0:T(8,128)(2,1)}, f32[3,8,128]{2,1,0:T(8,128)}, f32[384,1536]{1,0:T(8,128)}, f32[128,640]{1,0:T(8,128)}, f32[384,1536]{1,0:T(8,128)}) custom-call(s32[1]{0:T(128)S(6)} %copy.20.len_ref, s32[1]{0:T(128)} %bitcast.1.own_ref, bf16[16,24,24,128]{3,2,1,0:T(8,128)(2,1)} %copy-done.7, f32[1,128]{1,0:T(1,128)} %bitcast.31, ...), custom_call_target="tpu_custom_call" | custom-call | flops 24000000000 | bytes 1769472 | tf_op jit(solution)/shard_map/pallas_call | solution.py:279
  75.2 1.9 all-to-all-done.2.cells_ref
  77.2 5.6 %all-to-all-start = ((bf16[16,18,24,128]{3,2,1,0:T(8,128)(2,1)}), bf16[16,18,24,128]{3,2,1,0:T(8,128)(2,1)S(1)}, u32[]{:S(2)}, u32[]{:S(2)}) async-start(bf16[16,18,24,128]{3,2,1,0:T(8,128)(2,1)} %shard_map.144), calls=%async_computation | async-start | bytes 3538944 | tf_op jit(solution)/shard_map/all_to_all | solution.py:394
  82.8 27.4 %shard_map.149 = (bf16[16,15,24,128]{3,2,1,0:T(8,128)(2,1)}, f32[3,8,128]{2,1,0:T(8,128)}, f32[384,1536]{1,0:T(8,128)}, f32[128,640]{1,0:T(8,128)}) custom-call(s32[1]{0:T(128)S(6)} %copy.20.len_ref, s32[1]{0:T(128)} %bitcast.1.own_ref, bf16[16,18,24,128]{3,2,1,0:T(8,128)(2,1)} %all-to-all-done.2.cells_ref, f32[384,1536]{1,0:T(8,128)} %get-tuple-element.30.refs_0_, ...), custom_call_target="tpu_custom_call" | custom-call | flops 35999997952 | bytes 2654208 | tf_op jit(solution)/shard_map/pallas_call | solution.py:279
  110.2 5.9 %all-to-all-start.3 = ((bf16[16,15,24,128]{3,2,1,0:T(8,128)(2,1)}), bf16[16,15,24,128]{3,2,1,0:T(8,128)(2,1)S(1)}, u32[]{:S(2)}, u32[]{:S(2)}) async-start(bf16[16,15,24,128]{3,2,1,0:T(8,128)(2,1)} %get-tuple-element.39), calls=%async_computation.3 | async-start | bytes 2949120 | tf_op jit(solution)/shard_map/all_to_all | solution.py:394
  116.1 27.8 %shard_map.150 = (bf16[16,25,24,128]{3,2,1,0:T(8,128)(2,1)}, f32[3,8,128]{2,1,0:T(8,128)}) custom-call(s32[1]{0:T(128)S(6)} %copy.20.len_ref, s32[1]{0:T(128)} %bitcast.1.own_ref, bf16[16,18,24,128]{3,2,1,0:T(8,128)(2,1)} %copy-done.8, f32[384,1536]{1,0:T(8,128)} %get-tuple-element.30.refs_0_, f32[384,1536]{1,0:T(8,128)} %get-tuple-element.35.refs_1_, ...), custom_call_target="tpu_custom_call" | custom-call | flops 35999997952 | bytes 2654208 | tf_op jit(solution)/shard_map/pallas_call | solution.py:279
  144.0 36.8 %all_to_all.35.parts_ref.refs_1_ = bf16[16,25,24,128]{3,2,1,0:T(8,128)(2,1)S(1)} all-to-all(bf16[16,25,24,128]{3,2,1,0:T(8,128)(2,1)} %get-tuple-element.40), channel_id=1, replica_groups=mesh['dp'=8,'row'=16] {'row'}, dimensions={0} | all-to-all | bytes 4915200 | tf_op jit(solution)/shard_map/all_to_all | solution.py:394
  180.8 4.4 %shard_map.151 = (f32[4,24,384]{2,1,0:T(8,128)S(1)}, f32[6,8,128]{2,1,0:T(8,128)S(1)}) custom-call(bf16[24,384,128]{2,1,0:T(8,128)(2,1)S(1)} %bitcast.20, bf16[16,25,24,128]{3,2,1,0:T(8,128)(2,1)S(1)} %all_to_all.35.parts_ref.refs_1_, f32[1,128]{1,0:T(1,128)S(1)} %bitcast.36, f32[1,128]{1,0:T(1,128)S(1)} %bitcast.29, bf16[4,128]{1,0:T(4,128)(2,1)S(1)} %bitcast.24, ...), custom_call_target="tpu_custom_call" | custom-call | tf_op jit(solution)/shard_map/pallas_call | solution.py:448
  186.6 7.0 %all-to-all-start.5 = ((f32[8,6,8,128]{3,2,1,0:T(8,128)}), f32[8,6,8,128]{3,2,1,0:T(8,128)S(1)}, u32[]{:S(2)}, u32[]{:S(2)}) async-start(f32[8,6,8,128]{3,2,1,0:T(8,128)} %broadcast_in_dim.6), calls=%async_computation.5 | async-start | bytes 393216 | tf_op jit(solution)/shard_map/all_to_all | solution.py:394
  193.6 6.6 %shard_map.152.refs_2_ = bf16[24,384,128]{2,1,0:T(8,128)(2,1)} custom-call(bf16[24,384,128]{2,1,0:T(8,128)(2,1)} %bitcast.18, f32[4,24,384]{2,1,0:T(8,128)} %copy-done.6, f32[1,128]{1,0:T(1,128)} %bitcast.34, bf16[4,128]{1,0:T(4,128)(2,1)} %bitcast.22, bf16[16,15,24,128]{3,2,1,0:T(8,128)(2,1)} %copy-done.10, bf16[16,25,24,128]{3,2,1,0:T(8,128)(2,1)} %copy-done), custom_call_target="tpu_custom_call" | custom-call | flops 6000000000 | bytes 2359296 | tf_op jit(solution)/shard_map/pallas_call | solution.py:466
  200.8 0.8 broadcast_in_dim.8
  201.6 5.2 %all-to-all-start.6 = ((f32[16,6,8,128]{3,2,1,0:T(8,128)}), f32[16,6,8,128]{3,2,1,0:T(8,128)S(1)}, u32[]{:S(2)}, u32[]{:S(2)}) async-start(f32[16,6,8,128]{3,2,1,0:T(8,128)} %broadcast_in_dim.8), calls=%async_computation.6 | async-start | bytes 786432 | tf_op jit(solution)/shard_map/all_to_all | solution.py:394
  206.8 6.7 %shard_map.153 = bf16[24,384,128]{2,1,0:T(8,128)(2,1)} custom-call(bf16[24,384,128]{2,1,0:T(8,128)(2,1)} %bitcast.19, f32[4,24,384]{2,1,0:T(8,128)} %copy-done.6, f32[1,128]{1,0:T(1,128)} %bitcast.35, bf16[4,128]{1,0:T(4,128)(2,1)} %bitcast.23, bf16[16,15,24,128]{3,2,1,0:T(8,128)(2,1)} %copy-done.10, ...), custom_call_target="tpu_custom_call", output_to_operand_aliasing={{}: (6, {})} | custom-call | flops 6000000000 | bytes 2359296 | tf_op jit(solution)/shard_map/pallas_call | solution.py:466
  213.6 1.9 all-to-all-done.6.told_ref
  215.5 0.7 copy-done.9
  216.2 1.7 shard_map.154
  (31 shorter events, 2.7 us)
Async XLA Ops:
  9.8 7.5 %copy-start.11 = (bf16[128,512]{1,0:T(8,128)(2,1)S(1)}, bf16[128,512]{1,0:T(8,128)(2,1)}, u32[]{:S(2)}) copy-start(bf16[128,512]{1,0:T(8,128)(2,1)} %refs_6_.1) | copy-start | bytes 393220
  9.8 8.2 %copy-start.12 = (bf16[128,128]{1,0:T(8,128)(2,1)S(1)}, bf16[128,128]{1,0:T(8,128)(2,1)}, u32[]{:S(2)}) copy-start(bf16[128,128]{1,0:T(8,128)(2,1)} %param.17) | copy-start | bytes 98308
  9.8 37.7 %all-to-all-start.1 = ((bf16[16,24,24,128]{3,2,1,0:T(8,128)(2,1)}), bf16[16,24,24,128]{3,2,1,0:T(8,128)(2,1)S(1)}, u32[]{:S(2)}, u32[]{:S(2)}) async-start(bf16[16,24,24,128]{3,2,1,0:T(8,128)(2,1)} %shard_map.146), calls=%async_computation.1 | async-start | bytes 4718592 | tf_op jit(solution)/shard_map/all_to_all | solution.py:394
  47.5 6.3 %copy-start.7 = (bf16[16,24,24,128]{3,2,1,0:T(8,128)(2,1)}, bf16[16,24,24,128]{3,2,1,0:T(8,128)(2,1)S(1)}, u32[]{:S(2)}) copy-start(bf16[16,24,24,128]{3,2,1,0:T(8,128)(2,1)S(1)} %all-to-all-done.1.cells_ref) | copy-start | bytes 7077892
  47.5 29.7 %all-to-all-start.2 = ((bf16[16,18,24,128]{3,2,1,0:T(8,128)(2,1)}), bf16[16,18,24,128]{3,2,1,0:T(8,128)(2,1)}, u32[]{:S(2)}, u32[]{:S(2)}) async-start(bf16[16,18,24,128]{3,2,1,0:T(8,128)(2,1)} %shard_map.148), calls=%async_computation.2 | async-start | bytes 3538944 | tf_op jit(solution)/shard_map/all_to_all | solution.py:394
  77.2 33.0 %all-to-all-start = ((bf16[16,18,24,128]{3,2,1,0:T(8,128)(2,1)}), bf16[16,18,24,128]{3,2,1,0:T(8,128)(2,1)S(1)}, u32[]{:S(2)}, u32[]{:S(2)}) async-start(bf16[16,18,24,128]{3,2,1,0:T(8,128)(2,1)} %shard_map.144), calls=%async_computation | async-start | bytes 3538944 | tf_op jit(solution)/shard_map/all_to_all | solution.py:394
  110.2 5.9 %copy-start.8 = (bf16[16,18,24,128]{3,2,1,0:T(8,128)(2,1)}, bf16[16,18,24,128]{3,2,1,0:T(8,128)(2,1)S(1)}, u32[]{:S(2)}) copy-start(bf16[16,18,24,128]{3,2,1,0:T(8,128)(2,1)S(1)} %all-to-all-done.cells_ref) | copy-start | bytes 5308420
  110.2 33.7 %all-to-all-start.3 = ((bf16[16,15,24,128]{3,2,1,0:T(8,128)(2,1)}), bf16[16,15,24,128]{3,2,1,0:T(8,128)(2,1)S(1)}, u32[]{:S(2)}, u32[]{:S(2)}) async-start(bf16[16,15,24,128]{3,2,1,0:T(8,128)(2,1)} %get-tuple-element.39), calls=%async_computation.3 | async-start | bytes 2949120 | tf_op jit(solution)/shard_map/all_to_all | solution.py:394
  143.9 36.8 %copy-start.10 = (bf16[16,15,24,128]{3,2,1,0:T(8,128)(2,1)}, bf16[16,15,24,128]{3,2,1,0:T(8,128)(2,1)S(1)}, u32[]{:S(2)}) copy-start(bf16[16,15,24,128]{3,2,1,0:T(8,128)(2,1)S(1)} %all-to-all-done.3.refs_0_) | copy-start | bytes 4423684
  143.9 36.8 %copy-start.1 = (bf16[1,24,384,128]{3,2,1,0:T(8,128)(2,1)S(1)}, bf16[1,24,384,128]{3,2,1,0:T(8,128)(2,1)}, u32[]{:S(2)}) copy-start(bf16[1,24,384,128]{3,2,1,0:T(8,128)(2,1)} %param.9) | copy-start | bytes 7077892
  143.9 36.8 %copy-start.2 = (f32[3,8,128]{2,1,0:T(8,128)S(1)}, f32[3,8,128]{2,1,0:T(8,128)}, u32[]{:S(2)}) copy-start(f32[3,8,128]{2,1,0:T(8,128)} %get-tuple-element.41.sacc_ref) | copy-start | bytes 36868
  143.9 36.8 %copy-start.3 = (bf16[128,4]{0,1:T(4,128)(2,1)S(1)}, bf16[128,4]{0,1:T(4,128)(2,1)}, u32[]{:S(2)}) copy-start(bf16[128,4]{0,1:T(4,128)(2,1)} %param.16) | copy-start | bytes 3076
  144.0 36.8 %copy-start.4 = (f32[128]{0:T(128)S(1)}, f32[128]{0:T(128)}, u32[]{:S(2)}) copy-start(f32[128]{0:T(128)} %param.13) | copy-start | bytes 1540
  144.0 36.8 %copy-start.5 = (f32[128]{0:T(128)S(1)}, f32[128]{0:T(128)}, u32[]{:S(2)}) copy-start(f32[128]{0:T(128)} %param.12) | copy-start | bytes 1540
  180.7 4.5 %copy-start = (bf16[16,25,24,128]{3,2,1,0:T(8,128)(2,1)}, bf16[16,25,24,128]{3,2,1,0:T(8,128)(2,1)S(1)}, u32[]{:S(2)}) copy-start(bf16[16,25,24,128]{3,2,1,0:T(8,128)(2,1)S(1)} %all_to_all.35.parts_ref.refs_1_) | copy-start | bytes 7372804
  185.2 0.7 copy-start.6
  186.6 14.2 %all-to-all-start.5 = ((f32[8,6,8,128]{3,2,1,0:T(8,128)}), f32[8,6,8,128]{3,2,1,0:T(8,128)S(1)}, u32[]{:S(2)}, u32[]{:S(2)}) async-start(f32[8,6,8,128]{3,2,1,0:T(8,128)} %broadcast_in_dim.6), calls=%async_computation.5 | async-start | bytes 393216 | tf_op jit(solution)/shard_map/all_to_all | solution.py:394
  201.6 13.9 %all-to-all-start.6 = ((f32[16,6,8,128]{3,2,1,0:T(8,128)}), f32[16,6,8,128]{3,2,1,0:T(8,128)S(1)}, u32[]{:S(2)}, u32[]{:S(2)}) async-start(f32[16,6,8,128]{3,2,1,0:T(8,128)} %broadcast_in_dim.8), calls=%async_computation.6 | async-start | bytes 786432 | tf_op jit(solution)/shard_map/all_to_all | solution.py:394
  215.5 0.7 copy-start.9
where the time goes:
time: 222 us; the launch traced here: 218 us
  Pallas kernels  113 us (51%)
  starting transfers between devices  37.6 us (17%)
  blocking collectives  36.8 us (17%)
  waiting for transfers between devices  24.6 us (11%)
  local copies, waits for them, and re-layouts  4.42 us (2%)
    pallas_call x3, Pallas kernels, columns_call(): pl.pallas_call(functools.partial(columns_kernel, heads, first, last, col0...  76.6 us
    all_to_all x6, starting transfers between devices, exchange(): return lax.all_to_all(a, axis, 0, 0)  37.6 us
    all_to_all x1, blocking collectives, exchange(): return lax.all_to_all(a, axis, 0, 0)  36.8 us
    all_to_all x6, waiting for transfers between devices, exchange(): return lax.all_to_all(a, axis, 0, 0)  24.6 us
    pallas_call x2, Pallas kernels, norm_back(): pl.pallas_call(functools.partial(norm_back_kernel, first), grid=(steps,),...  13.3 us
    pallas_call x3, Pallas kernels, send(): pl.pallas_call(functools.partial(send_kernel, start, count), grid=(src //...  11.6 us
    pallas_call x1, Pallas kernels, body(): pl.pallas_call(functools.partial(logits_kernel, heads), grid=(rows // lin...  5.39 us
  transfers between devices with their start and end apart: 6, of which 4 were waited for; matrix products, arithmetic and copies ran while one was open for 1% of the time, Pallas kernels for 45%

commit v1 on v0

--- a/solution.py
+++ b/solution.py
@@ -300,10 +300,19 @@
     )(length, own, *inputs)
 
 
-def side_kernel(heads, pair_ref, parts_ref, gain_ref, shift_ref, wbt_ref, sacc_ref, sum_ref, share_ref):
+def normed_kernel(pair_ref, gain_ref, shift_ref, out_ref):
     rows, n, channels = pair_ref.shape
+    xhat, _ = norm_parts(pair_ref[...].astype(F32).reshape(rows * n, channels).astype(BF))
+    normed = xhat * gain_ref[...] + shift_ref[...]
+    out_ref[:, :, :channels] = normed.reshape(rows, n, channels).astype(BF)
+    out_ref[:, :, channels:] = xhat.reshape(rows, n, channels).astype(BF)
+
+
+def side_kernel(heads, normed_ref, parts_ref, wbt_ref, sacc_ref, sum_ref, told_ref):
+    rows, n, channels = parts_ref.shape[2], sum_ref.shape[2], parts_ref.shape[3]
     thirds = n // channels
     slots = heads * thirds
+    share_ref = told_ref.at[0]
     total = jnp.sum(parts_ref[:, :slots].astype(F32), axis=0).astype(BF).astype(F32)
     for h in range(heads):
         for t in range(thirds):
@@ -317,11 +326,9 @@
     stats = jnp.zeros((heads, 2 * channels), F32)
     flat = jnp.zeros((heads, n), F32)
     for r in range(rows):
-        xhat, _ = norm_parts(pair_ref[r])
-        normed = (xhat * gain_ref[...] + shift_ref[...]).astype(BF)
         own = sum_ref[:, r, :]
         flat = flat + own
-        stats = stats + dot(own.astype(BF), jnp.concatenate([normed, xhat.astype(BF)], axis=1))
+        stats = stats + dot(own.astype(BF), normed_ref[r])
     wide = wbt_ref[...].astype(F32)
     share_ref[5, 0:1, :] = jnp.sum(sacc_ref[0], axis=0, keepdims=True)
     gain_part = wide * stats[:, channels:]
@@ -332,6 +339,8 @@
     share_ref[5, 2:3, :] = shift_all + jnp.sum(shift_part, axis=0, keepdims=True)
     share_ref[5, 3 : 3 + heads, :] = stats[:, :channels]
     share_ref[5, 3 + heads :, :] = jnp.zeros((5 - heads, channels), F32)
+    for d in range(1, told_ref.shape[0]):
+        told_ref[d] = share_ref[...]
 
 
 def norm_back_kernel(first, pair_ref, sums_ref, gain_ref, wbt_ref, *refs):
@@ -409,6 +418,18 @@
         compiler_params=pltpu.CompilerParams(vmem_limit_bytes=60 * MIB),
     )(pair, gain, shift, wbt)
     many = src // 2
+    both = pl.pallas_call(
+        normed_kernel,
+        grid=(rows // lines,),
+        in_specs=[pl.BlockSpec((lines, n, channels), lambda j: (j, 0, 0))]
+        + [whole(a.shape) for a in (gain, shift)],
+        out_specs=pl.BlockSpec((lines, n, 2 * channels), lambda j: (j, 0, 0)),
+        out_shape=jax.ShapeDtypeStruct((rows, n, 2 * channels), BF),
+        compiler_params=pltpu.CompilerParams(vmem_limit_bytes=60 * MIB),
+        cost_estimate=pl.CostEstimate(
+            flops=5 * 10**9, bytes_accessed=6 * pair.size, transcendentals=0
+        ),
+    )(pair, gain, shift)
     cells = pl.BlockSpec((rows, many * rows, channels), lambda j: (0, j, 0))
 
     def send(start, count, extra):
@@ -445,21 +466,22 @@
     bundle = exchange(out)
     back = (early, bundle)
 
+    copies = lax.axis_size("dp")
     sums, share = pl.pallas_call(
         functools.partial(side_kernel, heads),
         grid=(1,),
         in_specs=[
-            whole(pair.shape),
+            whole(both.shape),
             pl.BlockSpec((src, slots + SHARES, rows, channels), lambda j: (0, 0, 0, 0)),
         ]
-        + [whole(a.shape) for a in (gain, shift, wbt, sacc)],
-        out_specs=[whole((heads, rows, n)), whole((6, 8, channels))],
+        + [whole(a.shape) for a in (wbt, sacc)],
+        out_specs=[whole((heads, rows, n)), whole((copies, 6, 8, channels))],
         out_shape=[
             jax.ShapeDtypeStruct((heads, rows, n), F32),
-            jax.ShapeDtypeStruct((6, 8, channels), F32),
+            jax.ShapeDtypeStruct((copies, 6, 8, channels), F32),
         ],
         compiler_params=pltpu.CompilerParams(vmem_limit_bytes=40 * MIB),
-    )(pair, bundle, gain, shift, wbt, sacc)
+    )(both, bundle, wbt, sacc)
     def norm_back(first, steps, *written):
         place = lambda j: (0, j + first, 0)
         inputs = (pair, sums, gain, wbt, *back)
@@ -481,7 +503,7 @@
         )(*inputs, *written)
 
     blocks = n // tile
-    share = tell(share, "dp")
+    share = exchange(share, "dp")
     pair_grad = norm_back(0, blocks // 2)
     share, pair_grad = lax.optimization_barrier((share, pair_grad))
     told = tell(jnp.sum(share, axis=0), "row")

time: 222 us -> 225 us (1.014)
  blocking collectives: 36.8 us -> 0 us
  waiting for transfers between devices: 24.6 us -> 50.2 us
  starting transfers between devices: 37.6 us -> 44.7 us
  local copies, waits for them, and re-layouts: 4.42 us -> 8.12 us
  Pallas kernels: 113 us -> 116 us
    all_to_all x1 -> x0, blocking collectives: 36.8 us -> none  [exchange(): return lax.all_to_all(a, axis, 0, 0)]
    all_to_all x6 -> x7, waiting for transfers between devices: 24.6 us -> 50.2 us  [exchange(): return lax.all_to_all(a, axis, 0, 0)]
    all_to_all x6 -> x7, starting transfers between devices: 37.6 us -> 44.7 us  [exchange(): return lax.all_to_all(a, axis, 0, 0)]
    pallas_call x0 -> x1, Pallas kernels: none -> 6.11 us  [body(): pl.pallas_call(normed_kernel, grid=(rows // lines,), in_specs=[pl.BlockSp...]
    unnamed x28 -> x24, local copies, waits for them, and re-layouts: 2.93 us -> 7.35 us
    pallas_call x1, Pallas kernels: 4.42 us -> 1.7 us  [body(): pl.pallas_call(functools.partial(side_kernel, heads), grid=(1,), in_specs...]
  transfers between devices with their start and end apart: 6 -> 7, of which waited for: 4 -> 5; matrix products, arithmetic and copies ran while one was open for 1% -> 1% of each run, Pallas kernels for 45% -> 47%
where the time goes in v1:
time: 225 us; the launch traced here: 221 us
  Pallas kernels  116 us (52%)
  waiting for transfers between devices  50.2 us (22%)
  starting transfers between devices  44.7 us (20%)
  local copies, waits for them, and re-layouts  8.12 us (4%)
    pallas_call x3, Pallas kernels, columns_call(): pl.pallas_call(functools.partial(columns_kernel, heads, first, last, col0...  76.5 us
    all_to_all x7, waiting for transfers between devices, exchange(): return lax.all_to_all(a, axis, 0, 0)  50.2 us
    all_to_all x7, starting transfers between devices, exchange(): return lax.all_to_all(a, axis, 0, 0)  44.7 us
    pallas_call x2, Pallas kernels, norm_back(): pl.pallas_call(functools.partial(norm_back_kernel, first), grid=(steps,),...  13.3 us
    pallas_call x3, Pallas kernels, send(): pl.pallas_call(functools.partial(send_kernel, start, count), grid=(src //...  11.6 us
    unnamed x24, local copies, waits for them, and re-layouts  7.35 us
    pallas_call x1, Pallas kernels, body(): pl.pallas_call(normed_kernel, grid=(rows // lines,), in_specs=[pl.BlockSp...  6.11 us
    pallas_call x1, Pallas kernels, body(): pl.pallas_call(functools.partial(logits_kernel, heads), grid=(rows // lin...  5.39 us
  transfers between devices with their start and end apart: 7, of which 5 were waited for; matrix products, arithmetic and copies ran while one was open for 1% of the time, Pallas kernels for 47%

profile of v1, /device:TPU:1, one launch (start us, length us, event | category | flops | bytes accessed | tf_op | source)
XLA Modules:
  0.0 221.1 jit_solution(6340820268306143121)
XLA Ops:
  0.6 5.4 %shard_map.146.refs_0_ = f32[12,24,128]{2,1,0:T(8,128)} custom-call(bf16[24,384,128]{2,1,0:T(8,128)(2,1)} %bitcast.18, f32[1,128]{1,0:T(1,128)} %bitcast.36, f32[1,128]{1,0:T(1,128)} %bitcast.31, bf16[4,128]{1,0:T(4,128)(2,1)} %bitcast.14), custom_call_target="tpu_custom_call" | custom-call | tf_op jit(solution)/shard_map/pallas_call | solution.py:411
  6.0 3.8 %shard_map.147 = bf16[16,24,24,128]{3,2,1,0:T(8,128)(2,1)} custom-call(bf16[24,384,128]{2,1,0:T(8,128)(2,1)} %bitcast.19, bf16[24,384,128]{2,1,0:T(8,128)(2,1)} %bitcast.43, f32[12,24,128]{2,1,0:T(8,128)} %shard_map.146.refs_0_), custom_call_target="tpu_custom_call" | custom-call | flops 5000000000 | bytes 3538944 | tf_op jit(solution)/shard_map/pallas_call | solution.py:437
  9.8 7.5 %all-to-all-start.1 = ((bf16[16,24,24,128]{3,2,1,0:T(8,128)(2,1)}), bf16[16,24,24,128]{3,2,1,0:T(8,128)(2,1)S(1)}, u32[]{:S(2)}, u32[]{:S(2)}) async-start(bf16[16,24,24,128]{3,2,1,0:T(8,128)(2,1)} %shard_map.147), calls=%async_computation.1 | async-start | bytes 4718592 | tf_op jit(solution)/shard_map/all_to_all | solution.py:403
  19.4 3.9 %shard_map.149 = bf16[16,18,24,128]{3,2,1,0:T(8,128)(2,1)} custom-call(bf16[24,384,128]{2,1,0:T(8,128)(2,1)} %bitcast.20, bf16[24,384,128]{2,1,0:T(8,128)(2,1)} %bitcast.44), custom_call_target="tpu_custom_call" | custom-call | flops 5000000000 | bytes 3538944 | tf_op jit(solution)/shard_map/pallas_call | solution.py:437
  23.3 3.9 %shard_map.145 = bf16[16,18,24,128]{3,2,1,0:T(8,128)(2,1)} custom-call(bf16[24,384,128]{2,1,0:T(8,128)(2,1)} %bitcast.21, bf16[24,384,128]{2,1,0:T(8,128)(2,1)} %bitcast.45), custom_call_target="tpu_custom_call" | custom-call | flops 5000000000 | bytes 3538944 | tf_op jit(solution)/shard_map/pallas_call | solution.py:437
  27.2 20.3 %all-to-all-done.1.cells_ref = bf16[16,24,24,128]{3,2,1,0:T(8,128)(2,1)S(1)} async-done(((bf16[16,24,24,128]{3,2,1,0:T(8,128)(2,1)}), bf16[16,24,24,128]{3,2,1,0:T(8,128)(2,1)S(1)}, u32[]{:S(2)}, u32[]{:S(2)}) %all-to-all-start.1) | async-done | bytes 2359328 | tf_op jit(solution)/shard_map/all_to_all | solution.py:403
  47.5 6.3 %all-to-all-start.2 = ((bf16[16,18,24,128]{3,2,1,0:T(8,128)(2,1)}), bf16[16,18,24,128]{3,2,1,0:T(8,128)(2,1)}, u32[]{:S(2)}, u32[]{:S(2)}) async-start(bf16[16,18,24,128]{3,2,1,0:T(8,128)(2,1)} %shard_map.149), calls=%async_computation.2 | async-start | bytes 3538944 | tf_op jit(solution)/shard_map/all_to_all | solution.py:403
  53.8 21.4 %shard_map.148 = (bf16[16,6,24,128]{3,2,1,0:T(8,128)(2,1)}, f32[3,8,128]{2,1,0:T(8,128)}, f32[384,1536]{1,0:T(8,128)}, f32[128,640]{1,0:T(8,128)}, f32[384,1536]{1,0:T(8,128)}) custom-call(s32[1]{0:T(128)S(6)} %copy.20.len_ref, s32[1]{0:T(128)} %bitcast.3.own_ref, bf16[16,24,24,128]{3,2,1,0:T(8,128)(2,1)} %copy-done.5, f32[1,128]{1,0:T(1,128)} %bitcast.37, ...), custom_call_target="tpu_custom_call" | custom-call | flops 24000000000 | bytes 1769472 | tf_op jit(solution)/shard_map/pallas_call | solution.py:279
  75.2 2.0 all-to-all-done.2.cells_ref
  77.2 5.6 %all-to-all-start = ((bf16[16,18,24,128]{3,2,1,0:T(8,128)(2,1)}), bf16[16,18,24,128]{3,2,1,0:T(8,128)(2,1)S(1)}, u32[]{:S(2)}, u32[]{:S(2)}) async-start(bf16[16,18,24,128]{3,2,1,0:T(8,128)(2,1)} %shard_map.145), calls=%async_computation | async-start | bytes 3538944 | tf_op jit(solution)/shard_map/all_to_all | solution.py:403
  82.8 27.4 %shard_map.150 = (bf16[16,15,24,128]{3,2,1,0:T(8,128)(2,1)}, f32[3,8,128]{2,1,0:T(8,128)}, f32[384,1536]{1,0:T(8,128)}, f32[128,640]{1,0:T(8,128)}) custom-call(s32[1]{0:T(128)S(6)} %copy.20.len_ref, s32[1]{0:T(128)} %bitcast.3.own_ref, bf16[16,18,24,128]{3,2,1,0:T(8,128)(2,1)} %all-to-all-done.2.cells_ref, f32[384,1536]{1,0:T(8,128)} %get-tuple-element.30.refs_0_, ...), custom_call_target="tpu_custom_call" | custom-call | flops 35999997952 | bytes 2654208 | tf_op jit(solution)/shard_map/pallas_call | solution.py:279
  110.2 5.9 %all-to-all-start.3 = ((bf16[16,15,24,128]{3,2,1,0:T(8,128)(2,1)}), bf16[16,15,24,128]{3,2,1,0:T(8,128)(2,1)S(1)}, u32[]{:S(2)}, u32[]{:S(2)}) async-start(bf16[16,15,24,128]{3,2,1,0:T(8,128)(2,1)} %get-tuple-element.39), calls=%async_computation.3 | async-start | bytes 2949120 | tf_op jit(solution)/shard_map/all_to_all | solution.py:403
  116.2 27.7 %shard_map.151 = (bf16[16,25,24,128]{3,2,1,0:T(8,128)(2,1)}, f32[3,8,128]{2,1,0:T(8,128)}) custom-call(s32[1]{0:T(128)S(6)} %copy.20.len_ref, s32[1]{0:T(128)} %bitcast.3.own_ref, bf16[16,18,24,128]{3,2,1,0:T(8,128)(2,1)} %copy-done.6, f32[384,1536]{1,0:T(8,128)} %get-tuple-element.30.refs_0_, f32[384,1536]{1,0:T(8,128)} %get-tuple-element.35.refs_1_, ...), custom_call_target="tpu_custom_call" | custom-call | flops 35999997952 | bytes 2654208 | tf_op jit(solution)/shard_map/pallas_call | solution.py:279
  145.1 5.7 %all-to-all-start.4 = ((bf16[16,25,24,128]{3,2,1,0:T(8,128)(2,1)}), bf16[16,25,24,128]{3,2,1,0:T(8,128)(2,1)S(1)}, u32[]{:S(2)}, u32[]{:S(2)}) async-start(bf16[16,25,24,128]{3,2,1,0:T(8,128)(2,1)} %get-tuple-element.40), calls=%async_computation.4 | async-start | bytes 4915200 | tf_op jit(solution)/shard_map/all_to_all | solution.py:403
  150.8 6.1 %shard_map.144.normed_ref = bf16[24,384,256]{2,1,0:T(8,128)(2,1)} custom-call(bf16[24,384,128]{2,1,0:T(8,128)(2,1)} %bitcast.22, f32[1,128]{1,0:T(1,128)} %bitcast.40, f32[1,128]{1,0:T(1,128)} %bitcast.35), custom_call_target="tpu_custom_call" | custom-call | flops 5000000000 | bytes 7077888 | tf_op jit(solution)/shard_map/pallas_call | solution.py:421
  157.0 25.4 %all-to-all-done.4.parts_ref.refs_1_ = bf16[16,25,24,128]{3,2,1,0:T(8,128)(2,1)S(1)} async-done(((bf16[16,25,24,128]{3,2,1,0:T(8,128)(2,1)}), bf16[16,25,24,128]{3,2,1,0:T(8,128)(2,1)S(1)}, u32[]{:S(2)}, u32[]{:S(2)}) %all-to-all-start.4) | async-done | bytes 2457632 | tf_op jit(solution)/shard_map/all_to_all | solution.py:403
  182.4 3.2 %copy-done.1 = bf16[24,384,256]{2,1,0:T(8,128)(2,1)S(1)} copy-done((bf16[24,384,256]{2,1,0:T(8,128)(2,1)S(1)}, bf16[24,384,256]{2,1,0:T(8,128)(2,1)}, u32[]{:S(2)}) %copy-start.1) | copy-done | bytes 4718616
  185.6 1.7 shard_map.152
  188.0 7.0 %all-to-all-start.5 = ((f32[8,6,8,128]{3,2,1,0:T(8,128)}), f32[8,6,8,128]{3,2,1,0:T(8,128)S(1)}, u32[]{:S(2)}, u32[]{:S(2)}) async-start(f32[8,6,8,128]{3,2,1,0:T(8,128)} %get-tuple-element.44), calls=%async_computation.5 | async-start | bytes 393216 | tf_op jit(solution)/shard_map/all_to_all | solution.py:403
  195.0 6.6 %shard_map.153.refs_2_ = bf16[24,384,128]{2,1,0:T(8,128)(2,1)} custom-call(bf16[24,384,128]{2,1,0:T(8,128)(2,1)} %bitcast.23, f32[4,24,384]{2,1,0:T(8,128)} %copy-done.4, f32[1,128]{1,0:T(1,128)} %bitcast.41, bf16[4,128]{1,0:T(4,128)(2,1)} %bitcast.15, bf16[16,15,24,128]{3,2,1,0:T(8,128)(2,1)} %copy-done.8, bf16[16,25,24,128]{3,2,1,0:T(8,128)(2,1)} %copy-done), custom_call_target="tpu_custom_call" | custom-call | flops 6000000000 | bytes 2359296 | tf_op jit(solution)/shard_map/pallas_call | solution.py:488
  203.1 6.7 %all-to-all-start.6 = ((f32[16,6,8,128]{3,2,1,0:T(8,128)}), f32[16,6,8,128]{3,2,1,0:T(8,128)S(1)}, u32[]{:S(2)}, u32[]{:S(2)}) async-start(f32[16,6,8,128]{3,2,1,0:T(8,128)} %broadcast_in_dim.10), calls=%async_computation.6 | async-start | bytes 786432 | tf_op jit(solution)/shard_map/all_to_all | solution.py:403
  209.8 6.7 %shard_map.154 = bf16[24,384,128]{2,1,0:T(8,128)(2,1)} custom-call(bf16[24,384,128]{2,1,0:T(8,128)(2,1)} %bitcast.24, f32[4,24,384]{2,1,0:T(8,128)} %copy-done.4, f32[1,128]{1,0:T(1,128)} %bitcast.42, bf16[4,128]{1,0:T(4,128)(2,1)} %bitcast.16, bf16[16,15,24,128]{3,2,1,0:T(8,128)(2,1)} %copy-done.8, ...), custom_call_target="tpu_custom_call", output_to_operand_aliasing={{}: (6, {})} | custom-call | flops 6000000000 | bytes 2359296 | tf_op jit(solution)/shard_map/pallas_call | solution.py:488
  216.5 1.8 all-to-all-done.6.told_ref
  219.1 1.7 shard_map.155
  (28 shorter events, 5.6 us)
Async XLA Ops:
  9.8 7.5 %copy-start.9 = (bf16[128,512]{1,0:T(8,128)(2,1)S(1)}, bf16[128,512]{1,0:T(8,128)(2,1)}, u32[]{:S(2)}) copy-start(bf16[128,512]{1,0:T(8,128)(2,1)} %refs_6_.1) | copy-start | bytes 393220
  9.8 8.2 %copy-start.10 = (bf16[128,128]{1,0:T(8,128)(2,1)S(1)}, bf16[128,128]{1,0:T(8,128)(2,1)}, u32[]{:S(2)}) copy-start(bf16[128,128]{1,0:T(8,128)(2,1)} %param.17) | copy-start | bytes 98308
  9.8 37.7 %all-to-all-start.1 = ((bf16[16,24,24,128]{3,2,1,0:T(8,128)(2,1)}), bf16[16,24,24,128]{3,2,1,0:T(8,128)(2,1)S(1)}, u32[]{:S(2)}, u32[]{:S(2)}) async-start(bf16[16,24,24,128]{3,2,1,0:T(8,128)(2,1)} %shard_map.147), calls=%async_computation.1 | async-start | bytes 4718592 | tf_op jit(solution)/shard_map/all_to_all | solution.py:403
  47.5 6.3 %copy-start.5 = (bf16[16,24,24,128]{3,2,1,0:T(8,128)(2,1)}, bf16[16,24,24,128]{3,2,1,0:T(8,128)(2,1)S(1)}, u32[]{:S(2)}) copy-start(bf16[16,24,24,128]{3,2,1,0:T(8,128)(2,1)S(1)} %all-to-all-done.1.cells_ref) | copy-start | bytes 7077892
  47.5 29.7 %all-to-all-start.2 = ((bf16[16,18,24,128]{3,2,1,0:T(8,128)(2,1)}), bf16[16,18,24,128]{3,2,1,0:T(8,128)(2,1)}, u32[]{:S(2)}, u32[]{:S(2)}) async-start(bf16[16,18,24,128]{3,2,1,0:T(8,128)(2,1)} %shard_map.149), calls=%async_computation.2 | async-start | bytes 3538944 | tf_op jit(solution)/shard_map/all_to_all | solution.py:403
  77.2 33.0 %all-to-all-start = ((bf16[16,18,24,128]{3,2,1,0:T(8,128)(2,1)}), bf16[16,18,24,128]{3,2,1,0:T(8,128)(2,1)S(1)}, u32[]{:S(2)}, u32[]{:S(2)}) async-start(bf16[16,18,24,128]{3,2,1,0:T(8,128)(2,1)} %shard_map.145), calls=%async_computation | async-start | bytes 3538944 | tf_op jit(solution)/shard_map/all_to_all | solution.py:403
  110.2 5.9 %copy-start.6 = (bf16[16,18,24,128]{3,2,1,0:T(8,128)(2,1)}, bf16[16,18,24,128]{3,2,1,0:T(8,128)(2,1)S(1)}, u32[]{:S(2)}) copy-start(bf16[16,18,24,128]{3,2,1,0:T(8,128)(2,1)S(1)} %all-to-all-done.cells_ref) | copy-start | bytes 5308420
  110.2 33.7 %all-to-all-start.3 = ((bf16[16,15,24,128]{3,2,1,0:T(8,128)(2,1)}), bf16[16,15,24,128]{3,2,1,0:T(8,128)(2,1)S(1)}, u32[]{:S(2)}, u32[]{:S(2)}) async-start(bf16[16,15,24,128]{3,2,1,0:T(8,128)(2,1)} %get-tuple-element.39), calls=%async_computation.3 | async-start | bytes 2949120 | tf_op jit(solution)/shard_map/all_to_all | solution.py:403
  143.9 1.2 copy-start.8
  145.1 37.3 %all-to-all-start.4 = ((bf16[16,25,24,128]{3,2,1,0:T(8,128)(2,1)}), bf16[16,25,24,128]{3,2,1,0:T(8,128)(2,1)S(1)}, u32[]{:S(2)}, u32[]{:S(2)}) async-start(bf16[16,25,24,128]{3,2,1,0:T(8,128)(2,1)} %get-tuple-element.40), calls=%async_computation.4 | async-start | bytes 4915200 | tf_op jit(solution)/shard_map/all_to_all | solution.py:403
  150.8 31.5 %copy-start.2 = (f32[3,8,128]{2,1,0:T(8,128)S(1)}, f32[3,8,128]{2,1,0:T(8,128)}, u32[]{:S(2)}) copy-start(f32[3,8,128]{2,1,0:T(8,128)} %get-tuple-element.41.sacc_ref) | copy-start | bytes 36868
  150.8 31.5 %copy-start.3 = (bf16[128,4]{0,1:T(4,128)(2,1)S(1)}, bf16[128,4]{0,1:T(4,128)(2,1)}, u32[]{:S(2)}) copy-start(bf16[128,4]{0,1:T(4,128)(2,1)} %param.16) | copy-start | bytes 3076
  182.4 4.9 %copy-start = (bf16[16,25,24,128]{3,2,1,0:T(8,128)(2,1)}, bf16[16,25,24,128]{3,2,1,0:T(8,128)(2,1)S(1)}, u32[]{:S(2)}) copy-start(bf16[16,25,24,128]{3,2,1,0:T(8,128)(2,1)S(1)} %all-to-all-done.4.parts_ref.refs_1_) | copy-start | bytes 7372804
  182.4 3.2 %copy-start.1 = (bf16[24,384,256]{2,1,0:T(8,128)(2,1)S(1)}, bf16[24,384,256]{2,1,0:T(8,128)(2,1)}, u32[]{:S(2)}) copy-start(bf16[24,384,256]{2,1,0:T(8,128)(2,1)} %shard_map.144.normed_ref) | copy-start | bytes 14155780
  187.3 0.7 copy-start.4
  188.0 14.3 %all-to-all-start.5 = ((f32[8,6,8,128]{3,2,1,0:T(8,128)}), f32[8,6,8,128]{3,2,1,0:T(8,128)S(1)}, u32[]{:S(2)}, u32[]{:S(2)}) async-start(f32[8,6,8,128]{3,2,1,0:T(8,128)} %get-tuple-element.44), calls=%async_computation.5 | async-start | bytes 393216 | tf_op jit(solution)/shard_map/all_to_all | solution.py:403
  203.1 15.3 %all-to-all-start.6 = ((f32[16,6,8,128]{3,2,1,0:T(8,128)}), f32[16,6,8,128]{3,2,1,0:T(8,128)S(1)}, u32[]{:S(2)}, u32[]{:S(2)}) async-start(f32[16,6,8,128]{3,2,1,0:T(8,128)} %broadcast_in_dim.10), calls=%async_computation.6 | async-start | bytes 786432 | tf_op jit(solution)/shard_map/all_to_all | solution.py:403
  218.4 0.7 copy-start.7

commit v2 on v1

--- a/solution.py
+++ b/solution.py
@@ -480,7 +480,7 @@
             jax.ShapeDtypeStruct((heads, rows, n), F32),
             jax.ShapeDtypeStruct((copies, 6, 8, channels), F32),
         ],
-        compiler_params=pltpu.CompilerParams(vmem_limit_bytes=40 * MIB),
+        compiler_params=pltpu.CompilerParams(vmem_limit_bytes=60 * MIB),
     )(both, bundle, wbt, sacc)
     def norm_back(first, steps, *written):
         place = lambda j: (0, j + first, 0)

time: 225 us -> 226 us (level)
  Pallas kernels: 116 us -> 119 us
  local copies, waits for them, and re-layouts: 8.12 us -> 5.7 us
    pallas_call x1, Pallas kernels: 1.7 us -> 4.47 us  [body(): pl.pallas_call(functools.partial(side_kernel, heads), grid=(1,), in_specs...]
    unnamed x24 -> x16, local copies, waits for them, and re-layouts: 7.35 us -> 4.93 us
where the time goes in v2:
time: 226 us; the launch traced here: 221 us
  Pallas kernels  119 us (53%)
  waiting for transfers between devices  50.2 us (22%)
  starting transfers between devices  44.8 us (20%)
  local copies, waits for them, and re-layouts  5.7 us (3%)
    pallas_call x3, Pallas kernels, columns_call(): pl.pallas_call(functools.partial(columns_kernel, heads, first, last, col0...  76.6 us
    all_to_all x7, waiting for transfers between devices, exchange(): return lax.all_to_all(a, axis, 0, 0)  50.2 us
    all_to_all x7, starting transfers between devices, exchange(): return lax.all_to_all(a, axis, 0, 0)  44.8 us
    pallas_call x2, Pallas kernels, norm_back(): pl.pallas_call(functools.partial(norm_back_kernel, first), grid=(steps,),...  13.3 us
    pallas_call x3, Pallas kernels, send(): pl.pallas_call(functools.partial(send_kernel, start, count), grid=(src //...  11.6 us
    pallas_call x1, Pallas kernels, body(): pl.pallas_call(normed_kernel, grid=(rows // lines,), in_specs=[pl.BlockSp...  6.09 us
    pallas_call x1, Pallas kernels, body(): pl.pallas_call(functools.partial(logits_kernel, heads), grid=(rows // lin...  5.39 us
    unnamed x16, local copies, waits for them, and re-layouts  4.93 us
  transfers between devices with their start and end apart: 7, of which 5 were waited for; matrix products, arithmetic and copies ran while one was open for 1% of the time, Pallas kernels for 47%

profile of v2, /device:TPU:1, one launch (start us, length us, event | category | flops | bytes accessed | tf_op | source)
XLA Modules:
  0.0 221.4 jit_solution(11133259175928154855)
XLA Ops:
  0.6 5.4 %shard_map.146.refs_0_ = f32[12,24,128]{2,1,0:T(8,128)} custom-call(bf16[24,384,128]{2,1,0:T(8,128)(2,1)} %bitcast.14, f32[1,128]{1,0:T(1,128)} %bitcast.36, f32[1,128]{1,0:T(1,128)} %bitcast.31, bf16[4,128]{1,0:T(4,128)(2,1)} %bitcast.27), custom_call_target="tpu_custom_call" | custom-call | tf_op jit(solution)/shard_map/pallas_call | solution.py:411
  6.0 3.8 %shard_map.147 = bf16[16,24,24,128]{3,2,1,0:T(8,128)(2,1)} custom-call(bf16[24,384,128]{2,1,0:T(8,128)(2,1)} %bitcast.15, bf16[24,384,128]{2,1,0:T(8,128)(2,1)} %bitcast.43, f32[12,24,128]{2,1,0:T(8,128)} %shard_map.146.refs_0_), custom_call_target="tpu_custom_call" | custom-call | flops 5000000000 | bytes 3538944 | tf_op jit(solution)/shard_map/pallas_call | solution.py:437
  9.8 7.5 %all-to-all-start.1 = ((bf16[16,24,24,128]{3,2,1,0:T(8,128)(2,1)}), bf16[16,24,24,128]{3,2,1,0:T(8,128)(2,1)S(1)}, u32[]{:S(2)}, u32[]{:S(2)}) async-start(bf16[16,24,24,128]{3,2,1,0:T(8,128)(2,1)} %shard_map.147), calls=%async_computation.1 | async-start | bytes 4718592 | tf_op jit(solution)/shard_map/all_to_all | solution.py:403
  19.4 3.9 %shard_map.149 = bf16[16,18,24,128]{3,2,1,0:T(8,128)(2,1)} custom-call(bf16[24,384,128]{2,1,0:T(8,128)(2,1)} %bitcast.16, bf16[24,384,128]{2,1,0:T(8,128)(2,1)} %bitcast.44), custom_call_target="tpu_custom_call" | custom-call | flops 5000000000 | bytes 3538944 | tf_op jit(solution)/shard_map/pallas_call | solution.py:437
  23.3 3.9 %shard_map.145 = bf16[16,18,24,128]{3,2,1,0:T(8,128)(2,1)} custom-call(bf16[24,384,128]{2,1,0:T(8,128)(2,1)} %bitcast.17, bf16[24,384,128]{2,1,0:T(8,128)(2,1)} %bitcast.45), custom_call_target="tpu_custom_call" | custom-call | flops 5000000000 | bytes 3538944 | tf_op jit(solution)/shard_map/pallas_call | solution.py:437
  27.2 20.3 %all-to-all-done.1.cells_ref = bf16[16,24,24,128]{3,2,1,0:T(8,128)(2,1)S(1)} async-done(((bf16[16,24,24,128]{3,2,1,0:T(8,128)(2,1)}), bf16[16,24,24,128]{3,2,1,0:T(8,128)(2,1)S(1)}, u32[]{:S(2)}, u32[]{:S(2)}) %all-to-all-start.1) | async-done | bytes 2359328 | tf_op jit(solution)/shard_map/all_to_all | solution.py:403
  47.5 6.3 %all-to-all-start.2 = ((bf16[16,18,24,128]{3,2,1,0:T(8,128)(2,1)}), bf16[16,18,24,128]{3,2,1,0:T(8,128)(2,1)}, u32[]{:S(2)}, u32[]{:S(2)}) async-start(bf16[16,18,24,128]{3,2,1,0:T(8,128)(2,1)} %shard_map.149), calls=%async_computation.2 | async-start | bytes 3538944 | tf_op jit(solution)/shard_map/all_to_all | solution.py:403
  53.8 21.4 %shard_map.148 = (bf16[16,6,24,128]{3,2,1,0:T(8,128)(2,1)}, f32[3,8,128]{2,1,0:T(8,128)}, f32[384,1536]{1,0:T(8,128)}, f32[128,640]{1,0:T(8,128)}, f32[384,1536]{1,0:T(8,128)}) custom-call(s32[1]{0:T(128)S(6)} %copy.20.len_ref, s32[1]{0:T(128)} %bitcast.3.own_ref, bf16[16,24,24,128]{3,2,1,0:T(8,128)(2,1)} %copy-done.1, f32[1,128]{1,0:T(1,128)} %bitcast.37, ...), custom_call_target="tpu_custom_call" | custom-call | flops 24000000000 | bytes 1769472 | tf_op jit(solution)/shard_map/pallas_call | solution.py:279
  75.3 1.9 all-to-all-done.2.cells_ref
  77.2 5.6 %all-to-all-start = ((bf16[16,18,24,128]{3,2,1,0:T(8,128)(2,1)}), bf16[16,18,24,128]{3,2,1,0:T(8,128)(2,1)S(1)}, u32[]{:S(2)}, u32[]{:S(2)}) async-start(bf16[16,18,24,128]{3,2,1,0:T(8,128)(2,1)} %shard_map.145), calls=%async_computation | async-start | bytes 3538944 | tf_op jit(solution)/shard_map/all_to_all | solution.py:403
  82.8 27.4 %shard_map.150 = (bf16[16,15,24,128]{3,2,1,0:T(8,128)(2,1)}, f32[3,8,128]{2,1,0:T(8,128)}, f32[384,1536]{1,0:T(8,128)}, f32[128,640]{1,0:T(8,128)}) custom-call(s32[1]{0:T(128)S(6)} %copy.20.len_ref, s32[1]{0:T(128)} %bitcast.3.own_ref, bf16[16,18,24,128]{3,2,1,0:T(8,128)(2,1)} %all-to-all-done.2.cells_ref, f32[384,1536]{1,0:T(8,128)} %get-tuple-element.30.refs_0_, ...), custom_call_target="tpu_custom_call" | custom-call | flops 35999997952 | bytes 2654208 | tf_op jit(solution)/shard_map/pallas_call | solution.py:279
  110.2 5.9 %all-to-all-start.3 = ((bf16[16,15,24,128]{3,2,1,0:T(8,128)(2,1)}), bf16[16,15,24,128]{3,2,1,0:T(8,128)(2,1)S(1)}, u32[]{:S(2)}, u32[]{:S(2)}) async-start(bf16[16,15,24,128]{3,2,1,0:T(8,128)(2,1)} %get-tuple-element.39), calls=%async_computation.3 | async-start | bytes 2949120 | tf_op jit(solution)/shard_map/all_to_all | solution.py:403
  116.2 27.7 %shard_map.151 = (bf16[16,25,24,128]{3,2,1,0:T(8,128)(2,1)}, f32[3,8,128]{2,1,0:T(8,128)}) custom-call(s32[1]{0:T(128)S(6)} %copy.20.len_ref, s32[1]{0:T(128)} %bitcast.3.own_ref, bf16[16,18,24,128]{3,2,1,0:T(8,128)(2,1)} %copy-done.2, f32[384,1536]{1,0:T(8,128)} %get-tuple-element.30.refs_0_, f32[384,1536]{1,0:T(8,128)} %get-tuple-element.35.refs_1_, ...), custom_call_target="tpu_custom_call" | custom-call | flops 35999997952 | bytes 2654208 | tf_op jit(solution)/shard_map/pallas_call | solution.py:279
  145.1 5.7 %all-to-all-start.4 = ((bf16[16,25,24,128]{3,2,1,0:T(8,128)(2,1)}), bf16[16,25,24,128]{3,2,1,0:T(8,128)(2,1)S(1)}, u32[]{:S(2)}, u32[]{:S(2)}) async-start(bf16[16,25,24,128]{3,2,1,0:T(8,128)(2,1)} %get-tuple-element.40), calls=%async_computation.4 | async-start | bytes 4915200 | tf_op jit(solution)/shard_map/all_to_all | solution.py:403
  150.8 6.1 %shard_map.144.normed_ref = bf16[24,384,256]{2,1,0:T(8,128)(2,1)} custom-call(bf16[24,384,128]{2,1,0:T(8,128)(2,1)} %bitcast.18, f32[1,128]{1,0:T(1,128)} %bitcast.40, f32[1,128]{1,0:T(1,128)} %bitcast.35), custom_call_target="tpu_custom_call" | custom-call | flops 5000000000 | bytes 7077888 | tf_op jit(solution)/shard_map/pallas_call | solution.py:421
  156.9 25.5 %all-to-all-done.4.parts_ref.refs_1_ = bf16[16,25,24,128]{3,2,1,0:T(8,128)(2,1)S(1)} async-done(((bf16[16,25,24,128]{3,2,1,0:T(8,128)(2,1)}), bf16[16,25,24,128]{3,2,1,0:T(8,128)(2,1)S(1)}, u32[]{:S(2)}, u32[]{:S(2)}) %all-to-all-start.4) | async-done | bytes 2457632 | tf_op jit(solution)/shard_map/all_to_all | solution.py:403
  182.4 1.5 copy-done
  183.8 4.5 %shard_map.152 = (f32[4,24,384]{2,1,0:T(8,128)}, f32[8,6,8,128]{3,2,1,0:T(8,128)}) custom-call(bf16[24,384,256]{2,1,0:T(8,128)(2,1)} %shard_map.144.normed_ref, bf16[16,25,24,128]{3,2,1,0:T(8,128)(2,1)} %copy-done, bf16[4,128]{1,0:T(4,128)(2,1)} %bitcast.28, f32[3,8,128]{2,1,0:T(8,128)} %get-tuple-element.41.sacc_ref), custom_call_target="tpu_custom_call" | custom-call | tf_op jit(solution)/shard_map/pallas_call | solution.py:470
  188.3 7.0 %all-to-all-start.5 = ((f32[8,6,8,128]{3,2,1,0:T(8,128)}), f32[8,6,8,128]{3,2,1,0:T(8,128)S(1)}, u32[]{:S(2)}, u32[]{:S(2)}) async-start(f32[8,6,8,128]{3,2,1,0:T(8,128)} %get-tuple-element.44), calls=%async_computation.5 | async-start | bytes 393216 | tf_op jit(solution)/shard_map/all_to_all | solution.py:403
  195.4 6.6 %shard_map.153.refs_2_ = bf16[24,384,128]{2,1,0:T(8,128)(2,1)} custom-call(bf16[24,384,128]{2,1,0:T(8,128)(2,1)} %bitcast.19, f32[4,24,384]{2,1,0:T(8,128)} %get-tuple-element.42.sums_ref, f32[1,128]{1,0:T(1,128)} %bitcast.41, bf16[4,128]{1,0:T(4,128)(2,1)} %bitcast.29, bf16[16,15,24,128]{3,2,1,0:T(8,128)(2,1)} %copy-done.4, bf16[16,25,24,128]{3,2,1,0:T(8,128)(2,1)} %copy-done), custom_call_target="tpu_custom_call" | custom-call | flops 6000000000 | bytes 2359296 | tf_op jit(solution)/shard_map/pallas_call | solution.py:488
  203.4 6.7 %all-to-all-start.6 = ((f32[16,6,8,128]{3,2,1,0:T(8,128)}), f32[16,6,8,128]{3,2,1,0:T(8,128)S(1)}, u32[]{:S(2)}, u32[]{:S(2)}) async-start(f32[16,6,8,128]{3,2,1,0:T(8,128)} %broadcast_in_dim.10), calls=%async_computation.6 | async-start | bytes 786432 | tf_op jit(solution)/shard_map/all_to_all | solution.py:403
  210.2 6.7 %shard_map.154 = bf16[24,384,128]{2,1,0:T(8,128)(2,1)} custom-call(bf16[24,384,128]{2,1,0:T(8,128)(2,1)} %bitcast.20, f32[4,24,384]{2,1,0:T(8,128)} %get-tuple-element.42.sums_ref, f32[1,128]{1,0:T(1,128)} %bitcast.42, bf16[4,128]{1,0:T(4,128)(2,1)} %bitcast.30, bf16[16,15,24,128]{3,2,1,0:T(8,128)(2,1)} %copy-done.4, ...), custom_call_target="tpu_custom_call", output_to_operand_aliasing={{}: (6, {})} | custom-call | flops 6000000000 | bytes 2359296 | tf_op jit(solution)/shard_map/pallas_call | solution.py:488
  216.9 1.9 all-to-all-done.6.told_ref
  219.5 1.7 shard_map.155
  (20 shorter events, 4.9 us)
Async XLA Ops:
  9.8 7.5 %copy-start.5 = (bf16[128,512]{1,0:T(8,128)(2,1)S(1)}, bf16[128,512]{1,0:T(8,128)(2,1)}, u32[]{:S(2)}) copy-start(bf16[128,512]{1,0:T(8,128)(2,1)} %refs_6_.1) | copy-start | bytes 393220
  9.8 8.2 %copy-start.6 = (bf16[128,128]{1,0:T(8,128)(2,1)S(1)}, bf16[128,128]{1,0:T(8,128)(2,1)}, u32[]{:S(2)}) copy-start(bf16[128,128]{1,0:T(8,128)(2,1)} %param.17) | copy-start | bytes 98308
  9.8 37.7 %all-to-all-start.1 = ((bf16[16,24,24,128]{3,2,1,0:T(8,128)(2,1)}), bf16[16,24,24,128]{3,2,1,0:T(8,128)(2,1)S(1)}, u32[]{:S(2)}, u32[]{:S(2)}) async-start(bf16[16,24,24,128]{3,2,1,0:T(8,128)(2,1)} %shard_map.147), calls=%async_computation.1 | async-start | bytes 4718592 | tf_op jit(solution)/shard_map/all_to_all | solution.py:403
  47.5 6.3 %copy-start.1 = (bf16[16,24,24,128]{3,2,1,0:T(8,128)(2,1)}, bf16[16,24,24,128]{3,2,1,0:T(8,128)(2,1)S(1)}, u32[]{:S(2)}) copy-start(bf16[16,24,24,128]{3,2,1,0:T(8,128)(2,1)S(1)} %all-to-all-done.1.cells_ref) | copy-start | bytes 7077892
  47.5 29.7 %all-to-all-start.2 = ((bf16[16,18,24,128]{3,2,1,0:T(8,128)(2,1)}), bf16[16,18,24,128]{3,2,1,0:T(8,128)(2,1)}, u32[]{:S(2)}, u32[]{:S(2)}) async-start(bf16[16,18,24,128]{3,2,1,0:T(8,128)(2,1)} %shard_map.149), calls=%async_computation.2 | async-start | bytes 3538944 | tf_op jit(solution)/shard_map/all_to_all | solution.py:403
  77.2 33.0 %all-to-all-start = ((bf16[16,18,24,128]{3,2,1,0:T(8,128)(2,1)}), bf16[16,18,24,128]{3,2,1,0:T(8,128)(2,1)S(1)}, u32[]{:S(2)}, u32[]{:S(2)}) async-start(bf16[16,18,24,128]{3,2,1,0:T(8,128)(2,1)} %shard_map.145), calls=%async_computation | async-start | bytes 3538944 | tf_op jit(solution)/shard_map/all_to_all | solution.py:403
  110.2 5.9 %copy-start.2 = (bf16[16,18,24,128]{3,2,1,0:T(8,128)(2,1)}, bf16[16,18,24,128]{3,2,1,0:T(8,128)(2,1)S(1)}, u32[]{:S(2)}) copy-start(bf16[16,18,24,128]{3,2,1,0:T(8,128)(2,1)S(1)} %all-to-all-done.cells_ref) | copy-start | bytes 5308420
  110.2 33.6 %all-to-all-start.3 = ((bf16[16,15,24,128]{3,2,1,0:T(8,128)(2,1)}), bf16[16,15,24,128]{3,2,1,0:T(8,128)(2,1)S(1)}, u32[]{:S(2)}, u32[]{:S(2)}) async-start(bf16[16,15,24,128]{3,2,1,0:T(8,128)(2,1)} %get-tuple-element.39), calls=%async_computation.3 | async-start | bytes 2949120 | tf_op jit(solution)/shard_map/all_to_all | solution.py:403
  143.9 1.2 copy-start.4
  145.1 37.3 %all-to-all-start.4 = ((bf16[16,25,24,128]{3,2,1,0:T(8,128)(2,1)}), bf16[16,25,24,128]{3,2,1,0:T(8,128)(2,1)S(1)}, u32[]{:S(2)}, u32[]{:S(2)}) async-start(bf16[16,25,24,128]{3,2,1,0:T(8,128)(2,1)} %get-tuple-element.40), calls=%async_computation.4 | async-start | bytes 4915200 | tf_op jit(solution)/shard_map/all_to_all | solution.py:403
  182.4 1.5 copy-start
  188.3 14.3 %all-to-all-start.5 = ((f32[8,6,8,128]{3,2,1,0:T(8,128)}), f32[8,6,8,128]{3,2,1,0:T(8,128)S(1)}, u32[]{:S(2)}, u32[]{:S(2)}) async-start(f32[8,6,8,128]{3,2,1,0:T(8,128)} %get-tuple-element.44), calls=%async_computation.5 | async-start | bytes 393216 | tf_op jit(solution)/shard_map/all_to_all | solution.py:403
  203.4 15.3 %all-to-all-start.6 = ((f32[16,6,8,128]{3,2,1,0:T(8,128)}), f32[16,6,8,128]{3,2,1,0:T(8,128)S(1)}, u32[]{:S(2)}, u32[]{:S(2)}) async-start(f32[16,6,8,128]{3,2,1,0:T(8,128)} %broadcast_in_dim.10), calls=%async_computation.6 | async-start | bytes 786432 | tf_op jit(solution)/shard_map/all_to_all | solution.py:403
  218.7 0.7 copy-start.3
